TPU v7x, 256 devices: a whole 4x4x8 slice. The times are simulated.
256 devices in a mesh: frame: 64 (over x_lo, z, y), band: 4 (over x_hi, core).
Axes of the slice: x: 4 (x_hi: 2, x_lo: 2; x = x_hi * 2 + x_lo), y: 4, z: 8, core: 2. Of those that a mesh axis runs over, the one named last changes fastest.
Arguments:
- queries: bfloat16 [64, 4, 2, 64, 3328], P('frame', 'band'), may hold values from -16 to 16
- keys: bfloat16 [64, 4, 2, 64, 3328], P('frame', 'band'), may hold values from -4 to 4
- values: bfloat16 [64, 4, 2, 64, 3328], P('frame', 'band'), may hold values from -6 to 6
- grad_out: bfloat16 [64, 4, 2, 64, 3328], P('frame', 'band'), may hold values from -6 to 6
- windows: int32 [64, 4, 2, 8], P('frame', 'band'), may hold values from 0 to 511, as said below
Outputs:
- attn_out: bfloat16 [64, 4, 2, 64, 3328], P('frame', 'band')
- grad_query: bfloat16 [64, 4, 2, 64, 3328], P('frame', 'band')
- grad_key: bfloat16 [64, 4, 2, 64, 3328], P('frame', 'band')
- grad_value: bfloat16 [64, 4, 2, 64, 3328], P('frame', 'band')
Inputs may be any that keep to these rules, and one draw needn't show every extreme that they name: `windows`: entry 0 of each window is the query tile itself; the other 7 entries are distinct tiles of the same or an adjacent frame and of the same or an adjacent band, at any position along the width.
All inputs are finite; a program needn't handle non-finite values.
Results may differ from a plain program's by a relative error of at most 0.015.
Values may be sent and summed in bfloat16 or wider, within the bound.
A program may use at most 128 MiB of HBM per device.

v0:
```python
import jax
import jax.numpy as jnp
from jax import lax
from jax.sharding import PartitionSpec as P

HD = 128
WIN = 8


def with_halo(cells, sides, width):
    for axis, dim in sides:
        count = lax.axis_size(axis)
        ends = count - 1
        head = lax.slice_in_dim(cells, 0, width, axis=dim)
        tail = lax.slice_in_dim(cells, cells.shape[dim] - width, cells.shape[dim], axis=dim)
        cells = jnp.concatenate(
            [
                lax.ppermute(tail, axis, [(i, (i + 1) % count) for i in range(ends)]),
                cells,
                lax.ppermute(head, axis, [((i + 1) % count, i) for i in range(ends)]),
            ],
            axis=dim,
        )
    return cells


def passed_along(shard, axis, by):
    size = lax.axis_size(axis)
    pairs = [(i, i + by) for i in range(size) if 0 <= i + by < size]
    return lax.ppermute(shard, axis, pairs)


def put_columns(buffer, update, column):
    return lax.dynamic_update_slice_in_dim(buffer, update, column, buffer.ndim - 1)


def split_heads(tensor, column):
    portion = lax.dynamic_slice_in_dim(tensor, column, 2 * HD, tensor.ndim - 1)
    return portion.reshape(portion.shape[:-1] + (2, HD))


def pair_scores(query_pair, key_pair, scaling):
    return (
        jnp.einsum("tqhd,tkhd->thqk", query_pair, key_pair, preferred_element_type=jnp.float32)
        * scaling
    )


def pair_forward(query_pair, key_pair, scaling):
    scores = pair_scores(query_pair, key_pair, scaling)
    maxima = jnp.max(scores, axis=-1, keepdims=True)
    log_total = maxima + jnp.log(jnp.sum(jnp.exp(scores - maxima), axis=-1, keepdims=True))
    return (jnp.exp(scores - log_total), log_total)


def pair_output(weights, value_pair):
    return jnp.einsum(
        "thqk,tkhd->tqhd",
        weights.astype(jnp.bfloat16),
        value_pair,
        preferred_element_type=jnp.float32,
    ).astype(jnp.bfloat16)


def pair_deltas(grad_pair, attn_pair):
    deltas = jnp.sum(grad_pair.astype(jnp.float32) * attn_pair.astype(jnp.float32), axis=-1)
    return jnp.transpose(deltas, (0, 2, 1))[..., None]


def score_grads(weights, pairs, attn_pair, scaling):
    query_pair, key_pair, value_pair, grad_pair = pairs
    deltas = pair_deltas(grad_pair, attn_pair)
    grad_prob = jnp.einsum(
        "tqhd,tkhd->thqk", grad_pair, value_pair, preferred_element_type=jnp.float32
    )
    return (weights * (grad_prob - deltas) * scaling).astype(jnp.bfloat16)


def pair_backward(weights, pairs, attn_pair, scaling):
    query_pair, key_pair, value_pair, grad_pair = pairs
    prob_round = weights.astype(jnp.bfloat16)
    grad_score = score_grads(weights, pairs, attn_pair, scaling)
    grad_query = jnp.einsum(
        "thqk,tkhd->tqhd", grad_score, key_pair, preferred_element_type=jnp.float32
    ).astype(jnp.bfloat16)
    key_slots = jnp.einsum(
        "thqk,tqhd->tkhd", grad_score, query_pair, preferred_element_type=jnp.float32
    )
    value_slots = jnp.einsum(
        "thqk,tqhd->tkhd", prob_round, grad_pair, preferred_element_type=jnp.float32
    )
    return (grad_query, key_slots, value_slots)


def on_device(queries, keys, values, grad_out, windows):
    tile_count = queries.shape[2]
    tile_len = queries.shape[3]
    feature = queries.shape[4]
    pair_width = 2 * HD
    pair_count = feature // pair_width
    head_count = 2 * pair_count
    slot_count = tile_count * WIN
    scaling = HD ** (-0.5)
    stacked = jnp.stack((keys, values))
    nearby = with_halo(stacked, (("frame", 1), ("band", 2)), 1)
    nearby = nearby.reshape(2, 9 * tile_count, tile_len, feature)
    frame_here = lax.axis_index("frame")
    band_here = lax.axis_index("band")
    band_total = lax.axis_size("band")
    tile_ids = windows.reshape(slot_count)
    frame_of = tile_ids // (band_total * tile_count)
    band_of = tile_ids // tile_count % band_total
    local_slot = (
        (frame_of - frame_here + 1) * 3 + band_of - band_here + 1
    ) * tile_count + tile_ids % tile_count
    select = (local_slot[:, None] == jnp.arange(9 * tile_count, dtype=jnp.int32)[None, :]).astype(
        jnp.float32
    )
    slot_keys = jnp.take(nearby[0], local_slot, axis=0).reshape(tile_count, WIN * tile_len, feature)
    slot_values = jnp.take(nearby[1], local_slot, axis=0).reshape(
        tile_count, WIN * tile_len, feature
    )
    query_rows = queries.reshape(tile_count, tile_len, feature)
    grad_rows = grad_out.reshape(tile_count, tile_len, feature)
    zero_rows = jnp.zeros((tile_count, tile_len, feature), jnp.bfloat16)
    zero_parts = jnp.zeros((2, 9 * tile_count, tile_len, feature), jnp.bfloat16)
    zero_totals = jnp.zeros((tile_count, head_count, tile_len, 1), jnp.float32)

    def take_pairs(column):
        return tuple(
            (
                split_heads(tensor, column)
                for tensor in (query_rows, slot_keys, slot_values, grad_rows)
            )
        )

    def forward_step(head_pair, buffers):
        out_buffer, total_buffer = buffers
        column = head_pair * pair_width
        pairs = take_pairs(column)
        weights, log_total = pair_forward(pairs[0], pairs[1], scaling)
        attn_pair = pair_output(weights, pairs[2])
        out_buffer = put_columns(
            out_buffer, attn_pair.reshape(tile_count, tile_len, pair_width), column
        )
        total_buffer = lax.dynamic_update_slice_in_dim(total_buffer, log_total, 2 * head_pair, 1)
        return (out_buffer, total_buffer)

    def stored_weights(pairs, log_totals, head_pair):
        log_total = lax.dynamic_slice_in_dim(log_totals, 2 * head_pair, 2, 1)
        return jnp.exp(pair_scores(pairs[0], pairs[1], scaling) - log_total)

    def backward_pair(weights, pairs, attn_pair, column, grad_buffer, part_buffer):
        grad_query, key_slots, value_slots = pair_backward(weights, pairs, attn_pair, scaling)
        slots_both = jnp.stack((key_slots, value_slots)).reshape(
            2, slot_count, tile_len, pair_width
        )
        partial_value = jnp.einsum(
            "sc,asjw->acjw", select, slots_both, precision=lax.Precision.HIGHEST
        ).astype(jnp.bfloat16)
        grad_buffer = put_columns(
            grad_buffer, grad_query.reshape(tile_count, tile_len, pair_width), column
        )
        return (grad_buffer, put_columns(part_buffer, partial_value, column))

    attention, log_totals = lax.fori_loop(0, pair_count, forward_step, (zero_rows, zero_totals))

    def backward_step(head_pair, buffers):
        grad_buffer, part_buffer = buffers
        column = head_pair * pair_width
        pairs = take_pairs(column)
        weights = stored_weights(pairs, log_totals, head_pair)
        attn_pair = split_heads(attention, column)
        return backward_pair(weights, pairs, attn_pair, column, grad_buffer, part_buffer)

    grad_query, partials = lax.fori_loop(0, pair_count, backward_step, (zero_rows, zero_parts))
    partials = partials.reshape(2, 3, 3, tile_count, tile_len, feature)
    from_below = passed_along(partials[:, :, 2:3], "band", 1)
    from_above = passed_along(partials[:, :, 0:1], "band", -1)
    column_sums = (
        partials[:, :, 1:2].astype(jnp.float32)
        + from_below.astype(jnp.float32)
        + from_above.astype(jnp.float32)
    )
    from_before = passed_along(column_sums[:, 2:3].astype(jnp.bfloat16), "frame", 1).astype(
        jnp.float32
    )
    from_after = passed_along(column_sums[:, 0:1].astype(jnp.bfloat16), "frame", -1).astype(
        jnp.float32
    )
    summed = column_sums[:, 1:2] + from_before + from_after
    gradients = summed.astype(jnp.bfloat16)
    return (
        attention.reshape(queries.shape),
        grad_query.reshape(queries.shape),
        gradients[0],
        gradients[1],
    )


def solution(mesh):
    placed = (
        P("frame", "band", None, None, None),
        P("frame", "band", None, None, None),
        P("frame", "band", None, None, None),
        P("frame", "band", None, None, None),
        P("frame", "band", None, None),
    )
    return jax.shard_map(
        on_device,
        mesh=mesh,
        in_specs=placed,
        out_specs=(
            P("frame", "band", None, None, None),
            P("frame", "band", None, None, None),
            P("frame", "band", None, None, None),
            P("frame", "band", None, None, None),
        ),
        check_vma=False,
    )
```

profile of v0, /device:TPU:9, one launch (start us, length us, event | category | flops | bytes accessed | tf_op | source)
XLA Modules:
  0.0 552.5 jit_solution(135752834529461177)
XLA Ops:
  4.3 3.4 collective-permute-start
  7.7 34.7 %collective-permute-done.1 = bf16[2,1,1,2,64,3328]{5,4,3,2,1,0:T(8,128)(2,1)S(1)} collective-permute-done((bf16[2,1,1,2,64,3328]{5,4,3,2,1,0:T(8,128)(2,1)S(1)}, bf16[2,1,1,2,64,3328]{5,4,3,2,1,0:T(8,128)(2,1)S(1)}, u32[]{:S(2)}, u32[]{:S(2)}) %collective-permute-start.1) | collective-permute-done | bytes 1703968 | tf_op jit(solution)/shard_map/ppermute | solution.py:20
  43.0 4.7 pad_maximum_fusion.1
  47.7 4.7 collective-permute-start.3
  52.4 4.7 collective-permute-start.2
  57.3 54.2 %collective-permute-done.3 = bf16[2,3,1,2,64,3328]{5,4,3,2,1,0:T(8,128)(2,1)} collective-permute-done((bf16[2,3,1,2,64,3328]{5,4,3,2,1,0:T(8,128)(2,1)}, bf16[2,3,1,2,64,3328]{5,4,3,2,1,0:T(8,128)(2,1)}, u32[]{:S(2)}, u32[]{:S(2)}) %collective-permute-start.3) | collective-permute-done | bytes 5111840 | tf_op jit(solution)/shard_map/ppermute | solution.py:20
  112.7 5.5 pad_maximum_fusion
  118.3 5.6 %fusion.44 = (bf16[1,3,3,2,64,3328]{5,4,3,2,1,0:T(8,128)(2,1)}, bf16[1,3,3,2,64,3328]{5,4,3,2,1,0:T(8,128)(2,1)}) fusion(bf16[2,3,3,2,64,3328]{5,4,3,2,1,0:T(8,128)(2,1)S(1)} %pad_maximum_fusion), kind=kLoop, calls=%fused_computation.88 | loop fusion | bytes 30670848 | tf_op jit(solution)/shard_map/slice | solution.py:119
  123.8 7.0 %gather_fusion.1 = bf16[16,64,3328]{2,1,0:T(8,128)(2,1)} fusion(bf16[18,64,3328]{2,1,0:T(8,128)(2,1)} %bitcast.156, s32[1024]{0:T(1024)S(1)} %pad_clamp_fusion), kind=kCustom, calls=%fused_computation.1.clone | custom fusion | bytes 13631552 | tf_op jit(solution)/shard_map/jit(_take)/gather | solution.py:119
  130.8 7.0 %gather_fusion = bf16[16,64,3328]{2,1,0:T(8,128)(2,1)} fusion(bf16[18,64,3328]{2,1,0:T(8,128)(2,1)} %bitcast.155, s32[1024]{0:T(1024)S(1)} %pad_clamp_fusion), kind=kCustom, calls=%fused_computation.clone | custom fusion | bytes 13631552 | tf_op jit(solution)/shard_map/jit(_take)/gather | solution.py:120
  137.8 10.1 %broadcast_select_fusion = (bf16[16,64,3328]{2,1,0:T(8,128)(2,1)}, bf16[16,64,3328]{2,1,0:T(8,128)(2,1)}) fusion(bf16[16,64,3328]{2,1,0:T(8,128)(2,1)} %gather_fusion.1, pred[16]{0:T(512)(128)(4,1)S(1)} %get-tuple-element.380, bf16[16,64,3328]{2,1,0:T(8,128)(2,1)} %gather_fusion), kind=kLoop, calls=%fused_computation.59 | loop fusion | flops 6815744 | bytes 27262992 | tf_op jit(solution)/shard_map/jit(_take)/select_n | solution.py:119
  148.0 10.0 %copy.66 = bf16[2,512,3328]{1,2,0:T(8,128)(2,1)} copy(bf16[2,512,3328]{2,1,0:T(8,128)(2,1)} %bitcast.158) | data formatting | bytes 13631488 | tf_op jit(solution)/shard_map/while | solution.py:166
  157.9 10.0 %copy.65 = bf16[2,512,3328]{1,2,0:T(8,128)(2,1)} copy(bf16[2,512,3328]{2,1,0:T(8,128)(2,1)} %bitcast.157) | data formatting | bytes 13631488 | tf_op jit(solution)/shard_map/while | solution.py:166
  168.9 47.6 %while.31 = (s32[]{:T(128)}, bf16[2,64,3328]{2,1,0:T(8,128)(2,1)}, f32[2,26,64,1]{2,1,0,3:T(8,128)S(1)}, bf16[2,512,3328]{1,2,0:T(8,128)(2,1)}, bf16[2,64,3328]{...) while((s32[]{:T(128)}, bf16[2,64,3328]{2,1,0:T(8,128)(2,1)}, ...), condition=%wide.region_3.5_spmd, body=%wide.region_0.4_spmd.sunk | while | flops 67927808 | bytes 4993257 | solution.py:166
  217.5 7.2 %broadcast_in_dim.31.clone = bf16[2,18,64,3328]{3,2,1,0:T(8,128)(2,1)} broadcast(bf16[]{:T(256)} %constant.178.clone.1), dimensions={} | broadcast | bytes 15335426 | tf_op jit(solution)/shard_map/broadcast_in_dim | solution.py:126
  224.6 189.8 %while.32 = (s32[]{:T(128)}, bf16[2,64,3328]{2,1,0:T(8,128)(2,1)}, bf16[2,18,64,3328]{3,2,1,0:T(8,128)(2,1)}, bf16[2,512,3328]{1,2,0:T(8,128)(2,1)}, bf16[2,64,3...) while((s32[]{:T(128)}, bf16[2,64,3328]{2,1,0:T(8,128)(2,1)}, ...), condition=%wide.region_6.8_spmd.clone, body=%wide.region_4.7_spmd.clone.sunk | while | flops 283214144 | bytes 27729236 | solution.py:176
  414.4 7.1 %fusion.43 = (bf16[2,3,1,2,64,3328]{5,4,3,2,1,0:T(8,128)(2,1)}, bf16[2,3,1,2,64,3328]{5,4,3,2,1,0:T(8,128)(2,1)S(1)}) fusion(bf16[2,3,3,2,64,3328]{5,4,3,2,1,0:T(8,128)(2,1)} %bitcast.150), kind=kLoop, calls=%fused_computation.87 | loop fusion | bytes 20447232 | tf_op jit(solution)/shard_map/slice | solution.py:178
  421.5 5.9 %collective-permute-start.4 = (bf16[2,3,1,2,64,3328]{5,4,3,2,1,0:T(8,128)(2,1)}, bf16[2,3,1,2,64,3328]{5,4,3,2,1,0:T(8,128)(2,1)}, u32[]{:S(2)}, u32[]{:S(2)}) collective-permute-start(bf16[2,3,1,2,64,3328]{5,4,3,2,1,0:T(8,128)(2,1)} %get-tuple-element.390), channel_id=1, source_target_pairs={{0,1},{1,2},{2,3},{4,5},{5,6},{6,7},{8,9},{9,10},{10,11},{12,13},{... | collective-permute-start | bytes 15335432 | tf_op jit(solution)/shard_map/ppermute | solution.py:30
  429.3 53.6 %collective-permute-done.4 = bf16[2,3,1,2,64,3328]{5,4,3,2,1,0:T(8,128)(2,1)} collective-permute-done((bf16[2,3,1,2,64,3328]{5,4,3,2,1,0:T(8,128)(2,1)}, bf16[2,3,1,2,64,3328]{5,4,3,2,1,0:T(8,128)(2,1)}, u32[]{:S(2)}, u32[]{:S(2)}) %collective-permute-start.4) | collective-permute-done | bytes 5111840 | tf_op jit(solution)/shard_map/ppermute | solution.py:30
  483.0 5.7 %collective-permute-done.5 = bf16[2,3,1,2,64,3328]{5,4,3,2,1,0:T(8,128)(2,1)} collective-permute-done((bf16[2,3,1,2,64,3328]{5,4,3,2,1,0:T(8,128)(2,1)S(1)}, bf16[2,3,1,2,64,3328]{5,4,3,2,1,0:T(8,128)(2,1)}, u32[]{:S(2)}, u32[]{:S(2)}) %collective-permute-start.5) | collective-permute-done | bytes 5111840 | tf_op jit(solution)/shard_map/ppermute | solution.py:30
  488.7 13.0 %fusion.40 = (bf16[2,3,1,2,64,3328]{5,4,3,2,1,0:T(8,128)(2,1)}, f32[2,3,1,2,64,3328]{5,4,3,2,1,0:T(8,128)}) fusion(bf16[2,3,1,2,64,3328]{5,4,3,2,1,0:T(8,128)(2,1)} %collective-permute-done.5, bf16[2,3,1,2,64,3328]{5,4,3,2,1,0:T(8,128)(2,1)} %collective-permute-done.4, bf16[2,3,3,2,64,3328]{5,4,3,2,1,0:T(8,128)(2,1)} %bitcast.151), kind=kLoop, calls=%fused_computation.85 | loop fusion | flops 15335424 | bytes 30670848 | tf_op jit(solution)/shard_map/convert.2
  503.9 3.2 collective-permute-start.6
  509.3 17.2 %collective-permute-done.6 = bf16[2,1,1,2,64,3328]{5,4,3,2,1,0:T(8,128)(2,1)S(1)} collective-permute-done((bf16[2,1,1,2,64,3328]{5,4,3,2,1,0:T(8,128)(2,1)S(1)}, bf16[2,1,1,2,64,3328]{5,4,3,2,1,0:T(8,128)(2,1)S(1)}, u32[]{:S(2)}, u32[]{:S(2)}) %collective-permute-start.6) | collective-permute-done | bytes 1703968 | tf_op jit(solution)/shard_map/ppermute | solution.py:30
  526.4 22.2 %collective-permute-done.7 = bf16[2,1,1,2,64,3328]{5,4,3,2,1,0:T(8,128)(2,1)S(1)} collective-permute-done((bf16[2,1,1,2,64,3328]{5,4,3,2,1,0:T(8,128)(2,1)S(1)}, bf16[2,1,1,2,64,3328]{5,4,3,2,1,0:T(8,128)(2,1)S(1)}, u32[]{:S(2)}, u32[]{:S(2)}) %collective-permute-start.7) | collective-permute-done | bytes 1703968 | tf_op jit(solution)/shard_map/ppermute | solution.py:30
  (375 shorter events, 253.5 us)
Async XLA Ops:
  2.2 55.0 %copy-start.3 = (s32[1,1,2,8]{3,2,1,0:T(2,128)S(1)}, s32[1,1,2,8]{3,2,1,0:T(2,128)}, u32[]{:S(2)}) copy-start(s32[1,1,2,8]{3,2,1,0:T(2,128)} %param.15) | copy-start | bytes 196
  2.2 110.5 %copy-start = (bf16[1,1,2,64,3328]{4,3,2,1,0:T(8,128)(2,1)S(1)}, bf16[1,1,2,64,3328]{4,3,2,1,0:T(8,128)(2,1)}, u32[]{:S(2)}) copy-start(bf16[1,1,2,64,3328]{4,3,2,1,0:T(8,128)(2,1)} %param.13) | copy-start | bytes 2555908
  2.2 110.5 %copy-start.1 = (bf16[1,1,2,64,3328]{4,3,2,1,0:T(8,128)(2,1)S(1)}, bf16[1,1,2,64,3328]{4,3,2,1,0:T(8,128)(2,1)}, u32[]{:S(2)}) copy-start(bf16[1,1,2,64,3328]{4,3,2,1,0:T(8,128)(2,1)} %param.12) | copy-start | bytes 2555908
  2.2 40.1 %collective-permute-start.1 = (bf16[2,1,1,2,64,3328]{5,4,3,2,1,0:T(8,128)(2,1)S(1)}, bf16[2,1,1,2,64,3328]{5,4,3,2,1,0:T(8,128)(2,1)S(1)}, u32[]{:S(2)}, u32[]{:S(2)}) collective-permute-start(bf16[2,1,1,2,64,3328]{5,4,3,2,1,0:T(8,128)(2,1)S(1)} %pad_maximum_fusion.2), channel_id=1, source_target_pairs={{4,0},{8,4},{12,8},{16,12},{20,16},{24,20},{28,24},{32,28},{36,32}... | collective-permute-start | bytes 5111816 | tf_op jit(solution)/shard_map/ppermute | solution.py:20
  4.3 38.7 %collective-permute-start = (bf16[2,1,1,2,64,3328]{5,4,3,2,1,0:T(8,128)(2,1)S(1)}, bf16[2,1,1,2,64,3328]{5,4,3,2,1,0:T(8,128)(2,1)S(1)}, u32[]{:S(2)}, u32[]{:S(2)}) collective-permute-start(bf16[2,1,1,2,64,3328]{5,4,3,2,1,0:T(8,128)(2,1)S(1)} %pad_maximum_fusion.2), channel_id=1, source_target_pairs={{0,4},{4,8},{8,12},{12,16},{16,20},{20,24},{24,28},{28,32},{32,36}... | collective-permute-start | bytes 5111816 | tf_op jit(solution)/shard_map/ppermute | solution.py:18
  43.0 4.7 copy-start.2
  47.7 63.8 %collective-permute-start.3 = (bf16[2,3,1,2,64,3328]{5,4,3,2,1,0:T(8,128)(2,1)}, bf16[2,3,1,2,64,3328]{5,4,3,2,1,0:T(8,128)(2,1)}, u32[]{:S(2)}, u32[]{:S(2)}) collective-permute-start(bf16[2,3,1,2,64,3328]{5,4,3,2,1,0:T(8,128)(2,1)} %pad_maximum_fusion.1), channel_id=1, source_target_pairs={{1,0},{2,1},{3,2},{5,4},{6,5},{7,6},{9,8},{10,9},{11,10},{13,12},{... | collective-permute-start | bytes 15335432 | tf_op jit(solution)/shard_map/ppermute | solution.py:20
  52.4 60.3 %collective-permute-start.2 = (bf16[2,3,1,2,64,3328]{5,4,3,2,1,0:T(8,128)(2,1)}, bf16[2,3,1,2,64,3328]{5,4,3,2,1,0:T(8,128)(2,1)}, u32[]{:S(2)}, u32[]{:S(2)}) collective-permute-start(bf16[2,3,1,2,64,3328]{5,4,3,2,1,0:T(8,128)(2,1)} %pad_maximum_fusion.1), channel_id=1, source_target_pairs={{0,1},{1,2},{2,3},{4,5},{5,6},{6,7},{8,9},{9,10},{10,11},{12,13},{... | collective-permute-start | bytes 15335432 | tf_op jit(solution)/shard_map/ppermute | solution.py:18
  421.5 61.5 %collective-permute-start.4 = (bf16[2,3,1,2,64,3328]{5,4,3,2,1,0:T(8,128)(2,1)}, bf16[2,3,1,2,64,3328]{5,4,3,2,1,0:T(8,128)(2,1)}, u32[]{:S(2)}, u32[]{:S(2)}) collective-permute-start(bf16[2,3,1,2,64,3328]{5,4,3,2,1,0:T(8,128)(2,1)} %get-tuple-element.390), channel_id=1, source_target_pairs={{0,1},{1,2},{2,3},{4,5},{5,6},{6,7},{8,9},{9,10},{10,11},{12,13},{... | collective-permute-start | bytes 15335432 | tf_op jit(solution)/shard_map/ppermute | solution.py:30
  427.4 61.3 %collective-permute-start.5 = (bf16[2,3,1,2,64,3328]{5,4,3,2,1,0:T(8,128)(2,1)S(1)}, bf16[2,3,1,2,64,3328]{5,4,3,2,1,0:T(8,128)(2,1)}, u32[]{:S(2)}, u32[]{:S(2)}) collective-permute-start(bf16[2,3,1,2,64,3328]{5,4,3,2,1,0:T(8,128)(2,1)S(1)} %get-tuple-element.391), channel_id=1, source_target_pairs={{1,0},{2,1},{3,2},{5,4},{6,5},{7,6},{9,8},{10,9},{11,10},{13,12},{... | collective-permute-start | bytes 15335432 | tf_op jit(solution)/shard_map/ppermute | solution.py:30
  503.9 22.6 %collective-permute-start.6 = (bf16[2,1,1,2,64,3328]{5,4,3,2,1,0:T(8,128)(2,1)S(1)}, bf16[2,1,1,2,64,3328]{5,4,3,2,1,0:T(8,128)(2,1)S(1)}, u32[]{:S(2)}, u32[]{:S(2)}) collective-permute-start(bf16[2,1,1,2,64,3328]{5,4,3,2,1,0:T(8,128)(2,1)S(1)} %get-tuple-element.394), channel_id=1, source_target_pairs={{0,4},{4,8},{8,12},{12,16},{16,20},{20,24},{24,28},{28,32},{32,36}... | collective-permute-start | bytes 5111816 | tf_op jit(solution)/shard_map/ppermute | solution.py:30
  507.1 41.6 %collective-permute-start.7 = (bf16[2,1,1,2,64,3328]{5,4,3,2,1,0:T(8,128)(2,1)S(1)}, bf16[2,1,1,2,64,3328]{5,4,3,2,1,0:T(8,128)(2,1)S(1)}, u32[]{:S(2)}, u32[]{:S(2)}) collective-permute-start(bf16[2,1,1,2,64,3328]{5,4,3,2,1,0:T(8,128)(2,1)S(1)} %get-tuple-element.395), channel_id=1, source_target_pairs={{4,0},{8,4},{12,8},{16,12},{20,16},{24,20},{28,24},{32,28},{36,32}... | collective-permute-start | bytes 5111816 | tf_op jit(solution)/shard_map/ppermute | solution.py:30
where the time goes:
time: 561 us; the launch traced here: 553 us
  waiting for transfers between devices  189 us (34%)
  local copies, waits for them, and re-layouts  182 us (32%)
  matrix products  95.5 us (17%)
  other arithmetic  55 us (10%)
  starting transfers between devices  28 us (5%)
    ppermute x4, waiting for transfers between devices, passed_along(): return lax.ppermute(shard, axis, pairs)  98.7 us
    ppermute x2, waiting for transfers between devices, with_halo(): lax.ppermute(head, axis, [((i + 1) % count, i) for i in range(ends)])  88.9 us
    another operation x52, local copies, waits for them, and re-layouts, backward_pair(): jnp.stack((key_slots, value_slots))  37.8 us
    dot_general x13, matrix products, backward_pair(): jnp.einsum('sc,asjw->acjw', select, slots_both, precision=lax.Precision.H...  35.6 us
    dynamic_update_slice x39, local copies, waits for them, and re-layouts, put_columns(): lax.dynamic_update_slice_in_dim(buffer, update, column, buffer.ndim - 1)  34.6 us
    dynamic_slice x26, local copies, waits for them, and re-layouts, split_heads(): portion = lax.dynamic_slice_in_dim(tensor, column, 2 * HD, tensor.ndim - 1)  33.1 us
    dot_general x26, matrix products, pair_scores(): jnp.einsum('tqhd,tkhd->thqk', query_pair, key_pair, preferred_element_typ...  28.8 us
    while x2, local copies, waits for them, and re-layouts, on_device(): lax.fori_loop(0, pair_count, forward_step, (zero_rows, zero_totals))  20 us
  transfers between devices with their start and end apart: 8, of which 8 were waited for; matrix products, arithmetic and copies ran while one was open for 0% of the time, Pallas kernels for 0%

commit v1 on v0

v1 whole, which is shorter than its diff:
```python
import functools

import jax
import jax.numpy as jnp
from jax import lax
from jax.experimental import pallas as pl
from jax.experimental.pallas import tpu as pltpu
from jax.sharding import PartitionSpec as P

MESH = pl.DeviceIdType.MESH
HD = 128
TILE = 64
WT = 2
BANDS = 4
TILES = BANDS * WT
ROWS = WT * TILE
MASKED = -1e30
AHEAD = 4
LATER = 2
LAG = 3
HALO, RET = 0, 1


def swapped(band):
    return 2 * (band % 2) + band // 2


def dot_nt(a, b):
    return lax.dot_general(a, b, (((1,), (1,)), ((), ())), preferred_element_type=jnp.float32)


def dot_tn(a, b):
    return lax.dot_general(a, b, (((0,), (0,)), ((), ())), preferred_element_type=jnp.float32)


def dot_nn(a, b):
    return jnp.dot(a, b, preferred_element_type=jnp.float32)


def kernel(
    frames, heads,
    win_ref, q_in, k_in, v_in, g_in,
    o_out, dq_out, dk_out, dv_out,
    qb, gb, kb, vb, bias, own_k, own_v, acc_k, acc_v, send_k, send_v, back_k, back_v, o_b, dq_b, dk_b, dv_b,
    in_send, in_recv, in_local, halo_send, halo_recv, ret_send, ret_recv, out_send, out_recv, out_local, bias_send, bias_recv,
    relay, relay_send, relay_recv,
):
    chip_heads = heads // 2
    most = (chip_heads + 1) // 2
    f, b = lax.axis_index("frame"), lax.axis_index("band")
    has_prev, has_next = f > 0, f < frames - 1
    peers = (b + 1 - 2 * (b % 2), (b + 2) % BANDS, BANDS - 1 - b)

    middle = frames // 2

    def across(frame, band):
        return band + (frame // middle) * (swapped(band) - band)

    spare = 2 * most - chip_heads
    own_set = across(f, b)

    def at(frame):
        return frame, across(frame, own_set)

    def head_count(band):
        return most - spare * ((across(f, band) + 1) // 2 % 2)

    def columns(band, j):
        those = across(f, band)
        first = most * those - spare * (2 * those // 3)
        return pl.ds(pl.multiple_of((first + j) * HD, HD), HD)

    def tiles(band):
        return pl.ds(WT * band, WT)

    mine = head_count(b)
    in_refs = (k_in, v_in, q_in, g_in)
    out_refs = (o_out, dq_out, dk_out, dv_out)
    out_bufs = (o_b, dq_b, dk_b, dv_b)

    def landing(arr, j):
        return (kb.at[j, 1], vb.at[j, 1], qb.at[j], gb.at[j])[arr].at[tiles(b)]

    def in_copy(arr, j, n):
        return pltpu.make_async_remote_copy(
            src_ref=in_refs[arr].at[0, 0, :, :, columns(peers[n], j)],
            dst_ref=landing(arr, j),
            send_sem=in_send.at[arr, j, n],
            recv_sem=in_recv.at[arr, j, n],
            device_id=(f, peers[n]),
            device_id_type=MESH,
        )

    def in_own(arr, j):
        return pltpu.make_async_copy(
            in_refs[arr].at[0, 0, :, :, columns(b, j)], landing(arr, j), in_local.at[arr, j]
        )

    def start_in(arrs, j):
        for n in (1, 2, 0):
            @pl.when(j < head_count(peers[n]))
            def _():
                for arr in arrs:
                    in_copy(arr, j, n).start()

        @pl.when(j < mine)
        def _():
            for arr in arrs:
                in_own(arr, j).start()

    def wait_in(arrs, j):
        for arr in arrs:
            in_own(arr, j).wait()
            for n in range(3):
                in_copy(arr, j, n).wait_recv()

    detour = (0, frames - 1)
    ends = ((middle, middle - 1), (middle - 1, middle))

    def straight(arr, j):
        return (2 * j + arr) % 2 == 0

    def side_refs(kind, arr, j, side):
        if kind == HALO:
            buf = (kb, vb)[arr]
            return buf.at[j, 1], buf.at[j, 2 - 2 * side], halo_send.at[arr, j, side], halo_recv.at[arr, j, side]
        return (
            (send_k, send_v)[arr].at[j, side],
            (back_k, back_v)[arr].at[j, 1 - side],
            ret_send.at[arr, j, side],
            ret_recv.at[arr, j, side],
        )

    def side_copy(kind, arr, j, side):
        source, target, send, recv = side_refs(kind, arr, j, side)
        return pltpu.make_async_remote_copy(
            src_ref=source, dst_ref=target, send_sem=send, recv_sem=recv,
            device_id=at(f - 1 + 2 * side), device_id_type=MESH,
        )

    def relay_in(kind, arr, j, side, over):
        source, _, send, _ = side_refs(kind, arr, j, side)
        return pltpu.make_async_remote_copy(
            src_ref=source, dst_ref=relay.at[kind, arr, j, side], send_sem=send,
            recv_sem=relay_recv.at[kind, arr, j, side], device_id=at(over), device_id_type=MESH,
        )

    def relay_out(kind, arr, j, side):
        _, target, _, recv = side_refs(kind, arr, j, side)
        return pltpu.make_async_remote_copy(
            src_ref=relay.at[kind, arr, j, side], dst_ref=target, send_sem=relay_send.at[kind, arr, j, side],
            recv_sem=recv, device_id=at(ends[side][1]), device_id_type=MESH,
        )

    def pass_on(kind, j, act):
        for side in range(2):
            for arr in range(2):
                @pl.when((f == detour[kind]) & jnp.logical_not(straight(arr, j)))
                def _():
                    act(kind, arr, j, side)

    def relay_start(kind, arr, j, side):
        relay_in(kind, arr, j, side, f).wait_recv()
        relay_out(kind, arr, j, side).start()

    def relay_end(kind, arr, j, side):
        relay_out(kind, arr, j, side).wait_send()

    has = (has_prev, has_next)

    def start_sides(kind, j):
        for side in range(2):
            @pl.when(has[side] & (f != ends[side][0]))
            def _():
                for arr in range(2):
                    side_copy(kind, arr, j, side).start()

            for arr in range(2):
                @pl.when((f == ends[side][0]) & straight(arr, j))
                def _():
                    side_copy(kind, arr, j, side).start()

                @pl.when((f == ends[side][0]) & jnp.logical_not(straight(arr, j)))
                def _():
                    relay_in(kind, arr, j, side, detour[kind]).start()

    def wait_sides(kind, j):
        for side in range(2):
            @pl.when(has[1 - side])
            def _():
                for arr in range(2):
                    side_copy(kind, arr, j, side).wait_recv()

    def out_copy(arr, j, n):
        return pltpu.make_async_remote_copy(
            src_ref=out_bufs[arr].at[j, tiles(peers[n])],
            dst_ref=out_refs[arr].at[0, 0, :, :, columns(b, j)],
            send_sem=out_send.at[arr, j, n],
            recv_sem=out_recv.at[arr, j, n],
            device_id=(f, peers[n]),
            device_id_type=MESH,
        )

    def out_own(arr, j):
        return pltpu.make_async_copy(
            out_bufs[arr].at[j, tiles(b)], out_refs[arr].at[0, 0, :, :, columns(b, j)], out_local.at[arr, j]
        )

    def start_out(arrs, j):
        for n in (1, 2, 0):
            for arr in arrs:
                out_copy(arr, j, n).start()
        for arr in arrs:
            out_own(arr, j).start()

    def bias_copy(n):
        return pltpu.make_async_remote_copy(
            src_ref=bias.at[b],
            dst_ref=bias.at[b],
            send_sem=bias_send.at[n],
            recv_sem=bias_recv.at[n],
            device_id=(f, peers[n]),
            device_id_type=MESH,
        )

    barrier = pltpu.get_barrier_semaphore()
    for n in range(3):
        pl.semaphore_signal(barrier, inc=1, device_id=(f, peers[n]), device_id_type=MESH)
    for side in range(2):
        @pl.when(has[side])
        def _():
            pl.semaphore_signal(
                barrier, inc=1, device_id=at(f - 1 + 2 * side), device_id_type=MESH
            )

    partners = {}
    for side in range(2):
        for way in detour:
            for end in ends[side]:
                partners.setdefault(end, set()).add(way)
                partners.setdefault(way, set()).add(end)
    for here in sorted(partners):
        @pl.when(f == here)
        def _():
            for there in sorted(partners[here]):
                pl.semaphore_signal(barrier, inc=1, device_id=at(there), device_id_type=MESH)

    place = lax.broadcasted_iota(jnp.int32, (3 * TILES, ROWS), 0) + TILES * (f - 1)
    lane = lax.broadcasted_iota(jnp.int32, (3 * TILES, ROWS), 1)
    named = []
    for t in range(WT):
        hits = [jnp.where(place == win_ref[0, 0, t, slot], 1, 0) for slot in range(8)]
        named.append(functools.reduce(jnp.maximum, hits))
    named = jnp.where(lane < TILE, named[0], named[1])
    bias[b] = jnp.where(named == 1, 0.0, MASKED)

    greeted = {}
    for here in sorted({0, frames - 1, *partners}):
        count = 3 + (here > 0) + (here < frames - 1) + len(partners.get(here, ()))
        greeted.setdefault(count, []).append(here)
    special = f < 0
    for count, those in sorted(greeted.items()):
        among = functools.reduce(jnp.logical_or, [f == here for here in those])
        special = special | among

        @pl.when(among)
        def _():
            pl.semaphore_wait(barrier, count)

    @pl.when(jnp.logical_not(special))
    def _():
        pl.semaphore_wait(barrier, 5)

    start_in((0, 1), 0)
    for n in range(3):
        bias_copy(n).start()
    lax.fori_loop(1, most, lambda j, carry: (start_in((0, 1), j), carry)[1], 0)

    nothing = jnp.zeros((most, TILES, TILE, HD), jnp.bfloat16)
    for side in range(2):
        @pl.when(jnp.logical_not(has[side]))
        def _():
            kb[:, 2 * side] = nothing
            vb[:, 2 * side] = nothing
            back_k[:, side] = nothing
            back_v[:, side] = nothing

    for n in range(3):
        pltpu.make_async_remote_copy(
            src_ref=bias.at[b], dst_ref=bias.at[peers[n]], send_sem=bias_send.at[n], recv_sem=bias_recv.at[n],
            device_id=(f, peers[n]), device_id_type=MESH,
        ).wait_recv()

    scaling = HD**-0.5
    scaling2 = scaling * 1.4426950408889634

    def compute(j):
        for band in range(BANDS):
            low, high = max(0, band - 1), min(BANDS, band + 2)
            tile_count = WT * (high - low)
            keys_count = tile_count * TILE
            q = qb[j, WT * band : WT * band + WT].reshape(ROWS, HD)
            g = gb[j, WT * band : WT * band + WT].reshape(ROWS, HD)
            ks = [kb[j, fr, WT * low : WT * high].reshape(keys_count, HD) for fr in range(3)]
            vs = [vb[j, fr, WT * low : WT * high].reshape(keys_count, HD) for fr in range(3)]
            scores = []
            for fr in range(3):
                start = fr * TILES + WT * low
                part = (dot_nt(ks[fr], q) * scaling2).reshape(tile_count, TILE, ROWS)
                part = part + bias[band, start : start + tile_count][:, None, :]
                scores.append(part.reshape(keys_count, ROWS))
            top = functools.reduce(
                jnp.maximum, [jnp.max(part, axis=0, keepdims=True) for part in scores]
            )
            weights = [jnp.exp2(part - top) for part in scores]
            total = sum(jnp.sum(part, axis=0, keepdims=True) for part in weights)
            share = 1.0 / total
            weights = [part * share for part in weights]
            probs = [part.astype(jnp.bfloat16) for part in weights]
            out = sum(dot_tn(probs[fr], vs[fr]) for fr in range(3)).astype(jnp.bfloat16)
            o_b[j, WT * band : WT * band + WT] = out.reshape(WT, TILE, HD)
            product = g.astype(jnp.float32) * out.astype(jnp.float32)
            deltas = jnp.sum(product.T, axis=0, keepdims=True)
            grads = []
            for fr in range(3):
                grad_prob = dot_nt(vs[fr], g)
                grads.append((weights[fr] * ((grad_prob - deltas) * scaling)).astype(jnp.bfloat16))
            dq = sum(dot_tn(grads[fr], ks[fr]) for fr in range(3)).astype(jnp.bfloat16)
            dq_b[j, WT * band : WT * band + WT] = dq.reshape(WT, TILE, HD)
            old = ROWS * (min(BANDS, band + 1) if band > 0 else 0)
            for fr in range(3):
                for acc, own, left, right in ((acc_k, own_k, grads, q), (acc_v, own_v, probs, g)):
                    into = own.at[j] if fr == 1 else acc.at[fr // 2]
                    part = dot_nn(left[fr], right)
                    seen = max(0, old - low * ROWS)
                    if seen:
                        into[low * ROWS : low * ROWS + seen, :] += part[:seen]
                    if seen < keys_count:
                        into[low * ROWS + seen : high * ROWS, :] = part[seen:]
        for side in range(2):
            send_k[j, side] = acc_k[side].astype(jnp.bfloat16).reshape(TILES, TILE, HD)
            send_v[j, side] = acc_v[side].astype(jnp.bfloat16).reshape(TILES, TILE, HD)

    def finish(j):
        for own, back, out in ((own_k, back_k, dk_b), (own_v, back_v, dv_b)):
            full = own[j].reshape(TILES, TILE, HD) + back[j, 0].astype(jnp.float32)
            out[j] = (full + back[j, 1].astype(jnp.float32)).astype(jnp.bfloat16)

    def share_out(j, carry):
        @pl.when(j < mine)
        def _():
            wait_in((0, 1), j)
            start_sides(HALO, j)

        @pl.when((j >= LAG) & (j - LAG < mine))
        def _():
            pass_on(HALO, j - LAG, relay_start)

        @pl.when(j < most)
        def _():
            start_in((2, 3), j)

        return carry

    lax.fori_loop(0, most, share_out, 0)

    def attend(j, carry):
        @pl.when(j < mine)
        def _():
            wait_in((2, 3), j)
            wait_sides(HALO, j)
            compute(j)
            start_sides(RET, j)
            start_out((0, 1), j)

        rest = j + most - LAG

        @pl.when(rest < mine)
        def _():
            pass_on(HALO, rest, relay_start)

        @pl.when((j >= LATER) & (j - LATER < mine))
        def _():
            pass_on(RET, j - LATER, relay_start)

        return carry

    lax.fori_loop(0, most + LATER, attend, 0)

    def gather(j, carry):
        wait_sides(RET, j)
        finish(j)
        start_out((2, 3), j)
        return carry

    lax.fori_loop(0, mine, gather, 0)

    for n in range(3):
        bias_copy(n).wait_send()

    def drain(j, carry):
        for n in range(3):
            @pl.when(j < head_count(peers[n]))
            def _():
                for arr in range(4):
                    in_copy(arr, j, n).wait_send()
                    out_copy(arr, j, n).wait_recv()

        @pl.when(j < mine)
        def _():
            for arr in range(4):
                out_own(arr, j).wait()
                for n in range(3):
                    out_copy(arr, j, n).wait_send()
            for side in range(2):
                @pl.when(has[side])
                def _():
                    for arr in range(2):
                        side_copy(HALO, arr, j, side).wait_send()
                        side_copy(RET, arr, j, side).wait_send()
            pass_on(HALO, j, relay_end)
            pass_on(RET, j, relay_end)

        return carry

    lax.fori_loop(0, most, drain, 0)


def copy_kernel(*refs):
    held, sems = refs[-2:]
    count = len(refs) // 2 - 1
    parts = [(i, t) for i in range(count) for t in range(WT)]
    loads = [pltpu.make_async_copy(refs[i].at[0, 0, t], held.at[i, t], sems.at[0, i, t]) for i, t in parts]
    stores = [pltpu.make_async_copy(held.at[i, t], refs[count + i].at[0, 0, t], sems.at[1, i, t]) for i, t in parts]
    for load in loads:
        load.start()
    for load, store in zip(loads, stores):
        load.wait()
        store.start()
    for store in stores:
        store.wait()


def on_device(frames, queries, keys, values, grad_out, windows):
    heads = queries.shape[-1] // HD
    most = (heads // 2 + 1) // 2
    near = (most, TILES, TILE, HD)
    wide = (most, 3, TILES, TILE, HD)
    both = (most, 2, TILES, TILE, HD)
    bf16 = functools.partial(pltpu.VMEM, dtype=jnp.bfloat16)
    f32 = functools.partial(pltpu.VMEM, dtype=jnp.float32)
    rows = TILES * TILE
    dma = pltpu.SemaphoreType.DMA
    anywhere = pl.BlockSpec(memory_space=pl.ANY)
    results = pl.pallas_call(
        functools.partial(kernel, frames, heads),
        name="window_attention",
        out_shape=[jax.ShapeDtypeStruct(queries.shape, jnp.bfloat16)] * 4,
        in_specs=[pl.BlockSpec(memory_space=pltpu.SMEM)] + [anywhere] * 4,
        out_specs=[anywhere] * 4,
        scratch_shapes=[
            bf16(near), bf16(near), bf16(wide), bf16(wide), f32((BANDS, 3 * TILES, ROWS)),
            f32((most, rows, HD)), f32((most, rows, HD)), f32((2, rows, HD)), f32((2, rows, HD)),
            bf16(both), bf16(both), bf16(both), bf16(both),
            bf16(near), bf16(near), bf16(near), bf16(near),
            dma((4, most, 3)), dma((4, most, 3)), dma((4, most)),
            dma((2, most, 2)), dma((2, most, 2)), dma((2, most, 2)), dma((2, most, 2)),
            dma((4, most, 3)), dma((4, most, 3)), dma((4, most)), dma((3,)), dma((3,)),
            bf16((2, 2, most, 2, TILES, TILE, HD)), dma((2, 2, most, 2)), dma((2, 2, most, 2)),
        ],
        cost_estimate=pl.CostEstimate(flops=8 * 10**9, bytes_accessed=8 * 10**6, transcendentals=4 * 10**6),
        compiler_params=pltpu.CompilerParams(
            collective_id=0, has_side_effects=True, vmem_limit_bytes=56 * 2**20
        ),
    )(windows, queries, keys, values, grad_out)
    return pl.pallas_call(
        copy_kernel,
        name="copy_out",
        out_shape=[jax.ShapeDtypeStruct(queries.shape, jnp.bfloat16)] * 4,
        in_specs=[anywhere] * 4,
        out_specs=[anywhere] * 4,
        scratch_shapes=[bf16((4, *queries.shape[2:])), dma((2, 4, WT))],
    )(*results)


def solution(mesh):
    placed = P("frame", "band", None, None, None)
    return jax.shard_map(
        functools.partial(on_device, mesh.shape["frame"]),
        mesh=mesh,
        in_specs=(placed, placed, placed, placed, P("frame", "band", None, None)),
        out_specs=(placed, placed, placed, placed),
        check_vma=False,
    )
```

time: 561 us -> 115 us (0.20)
  the two profiles are of different devices: /device:TPU:9 before, /device:TPU:249 now
where the time goes in v1:
time: 115 us
  Pallas kernels  114 us (99%)
    pallas_call x1, Pallas kernels, on_device(): pl.pallas_call(functools.partial(kernel, frames, heads), name='window_att...  111 us
    pallas_call x1, Pallas kernels, on_device(): pl.pallas_call(copy_kernel, name='copy_out', out_shape=[jax.ShapeDtypeStr...  2.89 us

profile of v1, /device:TPU:249, one launch (start us, length us, event | category | flops | bytes accessed | tf_op | source)
XLA Modules:
  0.0 114.8 jit_solution(13124055439043650393)
XLA Ops:
  0.6 111.3 %window_attention.1 = (bf16[1,1,2,64,3328]{4,3,2,1,0:T(8,128)(2,1)}, bf16[1,1,2,64,3328]{4,3,2,1,0:T(8,128)(2,1)}, bf16[1,1,2,64,3328]{4,3,2,1,0:T(8,128)(2,1)}, bf16[1,1,2,64,3328]{4,3,2,1,0:T(8,128)(2,1)}) custom-call(s32[1,1,2,8]{3,2,1,0:T(2,128)} %win_ref.1, bf16[1,1,2,64,3328]{4,3,2,1,0:T(8,128)(2,1)} %q_in.1, bf16[1,1,2,64,3328]{4,3,2,1,0:T(8,128)(2,1)} %k_in.1, ...), custom_call_target="tpu_custom_call" | custom-call | flops 8000000000 | bytes 8000000 | tf_op jit(solution)/shard_map/window_attention/pallas_call | solution.py:455
  112.0 2.9 %copy_out.1 = (bf16[1,1,2,64,3328]{4,3,2,1,0:T(8,128)(2,1)}, bf16[1,1,2,64,3328]{4,3,2,1,0:T(8,128)(2,1)}, bf16[1,1,2,64,3328]{4,3,2,1,0:T(8,128)(2,1)}, bf16[1,1,2,64,3328]{4,3,2,1,0:T(8,128)(2,1)}) custom-call(bf16[1,1,2,64,3328]{4,3,2,1,0:T(8,128)(2,1)} %get-tuple-element.8.refs_0_, bf16[1,1,2,64,3328]{4,3,2,1,0:T(8,128)(2,1)} %get-tuple-element.9.refs_1_, ...), custom_call_target="tpu_custom_call" | custom-call | tf_op jit(solution)/shard_map/copy_out/pallas_call | solution.py:476

commit v2 on v1

v2 whole, which is shorter than its diff:
```python
import functools

import jax
import jax.numpy as jnp
from jax import lax
from jax.experimental import pallas as pl
from jax.experimental.pallas import tpu as pltpu
from jax.sharding import PartitionSpec as P

MESH = pl.DeviceIdType.MESH
HD = 128
TILE = 64
WT = 2
BANDS = 4
TILES = BANDS * WT
ROWS = WT * TILE
MASKED = -1e30
AHEAD = 4
HALO, RET = 0, 1


def dot_nt(a, b):
    return lax.dot_general(a, b, (((1,), (1,)), ((), ())), preferred_element_type=jnp.float32)


def dot_tn(a, b):
    return lax.dot_general(a, b, (((0,), (0,)), ((), ())), preferred_element_type=jnp.float32)


def dot_nn(a, b):
    return jnp.dot(a, b, preferred_element_type=jnp.float32)


def kernel(
    frames, heads,
    win_ref, q_in, k_in, v_in, g_in,
    o_out, dq_out, dk_out, dv_out,
    qb, gb, kb, vb, bias, own_k, own_v, acc_k, acc_v, send_k, send_v, back_k, back_v, o_b, dq_b, dk_b, dv_b,
    in_send, in_recv, in_local, halo_send, halo_recv, ret_send, ret_recv, out_send, out_recv, out_local, bias_send, bias_recv,
    bias_own,
):
    chip_heads = heads // 2
    most = (chip_heads + 1) // 2
    half = frames // 2
    f, b = lax.axis_index("frame"), lax.axis_index("band")
    x, i, c = 2 * (b // 2) + f // half, f % half, b % 2
    p = i + half * c
    has_prev, has_next = p > 0, p < frames - 1
    last = most - 1

    def device(x, i, c):
        return half * (x % 2) + i, 2 * (x // 2) + c

    def head_count(those, at_half):
        return most - (those + at_half) % 2

    def columns(those, j):
        head = chip_heads * (those // 2) + most * (those % 2) * (1 - j // last) + j
        return pl.ds(pl.multiple_of(head * HD, HD), HD)

    def tiles(band):
        return pl.ds(WT * band, WT)

    def holder(band):
        return device(2 * (band // 2) + c, i, band % 2)

    def attender(those):
        return device(those, i, x % 2)

    def self_holds(band):
        return (band % 2 == c) & (2 * (band // 2) + c == x)

    def self_attends(those):
        return (those == x) & (x % 2 == c)

    mine = head_count(x, c)
    in_refs = (k_in, v_in, q_in, g_in)
    out_refs = (o_out, dq_out, dk_out, dv_out)
    out_bufs = (o_b, dq_b, dk_b, dv_b)

    def landing(arr, j, band):
        return (kb.at[j, 1], vb.at[j, 1], qb.at[j], gb.at[j])[arr].at[tiles(band)]

    def in_copy(arr, j, those):
        return pltpu.make_async_remote_copy(
            src_ref=in_refs[arr].at[0, 0, :, :, columns(those, j)],
            dst_ref=landing(arr, j, b),
            send_sem=in_send.at[arr, j, those],
            recv_sem=in_recv.at[arr, j, b],
            device_id=attender(those),
            device_id_type=MESH,
        )

    def in_arrival(arr, j, band):
        return pltpu.make_async_remote_copy(
            src_ref=in_refs[arr].at[0, 0, :, :, columns(x, j)],
            dst_ref=landing(arr, j, band),
            send_sem=in_send.at[arr, j, x],
            recv_sem=in_recv.at[arr, j, band],
            device_id=holder(band),
            device_id_type=MESH,
        )

    def in_own(arr, j):
        return pltpu.make_async_copy(
            in_refs[arr].at[0, 0, :, :, columns(x, j)], landing(arr, j, b), in_local.at[arr, j]
        )

    def start_in(arrs, j):
        for n in range(4):
            those = (x + 2 + n) % 4

            @pl.when((j < head_count(those, x % 2)) & jnp.logical_not(self_attends(those)))
            def _():
                for arr in arrs:
                    in_copy(arr, j, those).start()

            @pl.when((j < head_count(those, x % 2)) & self_attends(those))
            def _():
                for arr in arrs:
                    in_own(arr, j).start()

    def wait_in(arrs, j, band):
        @pl.when(self_holds(band))
        def _():
            for arr in arrs:
                in_own(arr, j).wait()

        @pl.when(jnp.logical_not(self_holds(band)))
        def _():
            for arr in arrs:
                in_arrival(arr, j, band).wait_recv()

    def to_side(side, j):
        other = p - 1 + 2 * side
        between = (other // half - c) * (other // half - c)
        beside = between * (j // last) * (1 - 2 * (x % 2))
        return device(x + beside, other % half, other // half)

    def side_refs(kind, arr, j, side):
        if kind == HALO:
            buf = (kb, vb)[arr]
            return buf.at[j, 1], buf.at[j, 2 - 2 * side], halo_send.at[arr, j, side], halo_recv.at[arr, j, side]
        return (
            (send_k, send_v)[arr].at[j, side],
            (back_k, back_v)[arr].at[j, 1 - side],
            ret_send.at[arr, j, side],
            ret_recv.at[arr, j, side],
        )

    def piece(kind, arr, j, side, n):
        source, target, send, recv = side_refs(kind, arr, j, side)
        part = tiles(n) if kind == HALO else pl.ds(2 * WT * n, 2 * WT)
        return pltpu.make_async_remote_copy(
            src_ref=source.at[part], dst_ref=target.at[part], send_sem=send.at[n], recv_sem=recv.at[n],
            device_id=to_side(side, j), device_id_type=MESH,
        )

    has = (has_prev, has_next)

    def start_pieces(kind, j, n):
        for side in range(2):
            @pl.when(has[side])
            def _():
                for arr in range(2):
                    piece(kind, arr, j, side, n).start()

    def wait_pieces(kind, j, n):
        for side in range(2):
            @pl.when(has[1 - side])
            def _():
                for arr in range(2):
                    piece(kind, arr, j, side, n).wait_recv()

    def out_copy(arr, j, band):
        return pltpu.make_async_remote_copy(
            src_ref=out_bufs[arr].at[j, tiles(band)],
            dst_ref=out_refs[arr].at[0, 0, :, :, columns(x, j)],
            send_sem=out_send.at[arr, j, band],
            recv_sem=out_recv.at[arr, j, x],
            device_id=holder(band),
            device_id_type=MESH,
        )

    def out_arrival(arr, j, those):
        return pltpu.make_async_remote_copy(
            src_ref=out_bufs[arr].at[j, tiles(b)],
            dst_ref=out_refs[arr].at[0, 0, :, :, columns(those, j)],
            send_sem=out_send.at[arr, j, b],
            recv_sem=out_recv.at[arr, j, those],
            device_id=attender(those),
            device_id_type=MESH,
        )

    def out_own(arr, j):
        return pltpu.make_async_copy(
            out_bufs[arr].at[j, tiles(b)], out_refs[arr].at[0, 0, :, :, columns(x, j)], out_local.at[arr, j]
        )

    def start_out(arrs, j, bands):
        for band in bands:
            @pl.when(self_holds(band))
            def _():
                for arr in arrs:
                    out_own(arr, j).start()

            @pl.when(jnp.logical_not(self_holds(band)))
            def _():
                for arr in arrs:
                    out_copy(arr, j, band).start()

    def bias_copy(those):
        return pltpu.make_async_remote_copy(
            src_ref=bias_own,
            dst_ref=bias.at[b],
            send_sem=bias_send.at[those],
            recv_sem=bias_recv.at[b],
            device_id=attender(those),
            device_id_type=MESH,
        )

    def bias_arrival(band):
        return pltpu.make_async_remote_copy(
            src_ref=bias_own,
            dst_ref=bias.at[band],
            send_sem=bias_send.at[x],
            recv_sem=bias_recv.at[band],
            device_id=holder(band),
            device_id_type=MESH,
        )

    middle = ((p == half - 1) | (p == half)) & (frames > 2)
    barrier = pltpu.get_barrier_semaphore()
    for step in range(1, 8):
        place = (2 * x + c + step) % 8
        pl.semaphore_signal(barrier, inc=1, device_id=device(place // 2, i, place % 2), device_id_type=MESH)
    for side in range(2):
        @pl.when(has[side])
        def _():
            pl.semaphore_signal(barrier, inc=1, device_id=to_side(side, 0), device_id_type=MESH)

        @pl.when(p == half - side)
        def _():
            pl.semaphore_signal(barrier, inc=1, device_id=to_side(side, last), device_id_type=MESH)

    place = lax.broadcasted_iota(jnp.int32, (3 * TILES, ROWS), 0) + TILES * (f - 1)
    lane = lax.broadcasted_iota(jnp.int32, (3 * TILES, ROWS), 1)
    named = []
    for t in range(WT):
        hits = [jnp.where(place == win_ref[0, 0, t, slot], 1, 0) for slot in range(8)]
        named.append(functools.reduce(jnp.maximum, hits))
    named = jnp.where(lane < TILE, named[0], named[1])
    bias_own[...] = jnp.where(named == 1, 0.0, MASKED)

    edge = jnp.logical_not(has_prev & has_next)

    @pl.when(middle)
    def _():
        pl.semaphore_wait(barrier, 10)

    @pl.when(edge)
    def _():
        pl.semaphore_wait(barrier, 8)

    @pl.when(jnp.logical_not(middle | edge))
    def _():
        pl.semaphore_wait(barrier, 9)

    start_in((0, 1), 0)
    for n in range(4):
        @pl.when(jnp.logical_not(self_attends(n)))
        def _():
            bias_copy(n).start()

        @pl.when(self_attends(n))
        def _():
            bias[b] = bias_own[...]

    lax.fori_loop(1, most, lambda j, carry: (start_in((0, 1), j), carry)[1], 0)

    nothing = jnp.zeros((most, TILES, TILE, HD), jnp.bfloat16)
    for side in range(2):
        @pl.when(jnp.logical_not(has[side]))
        def _():
            kb[:, 2 * side] = nothing
            vb[:, 2 * side] = nothing
            back_k[:, side] = nothing
            back_v[:, side] = nothing

    for n in range(4):
        @pl.when(jnp.logical_not(self_holds(n)))
        def _():
            bias_arrival(n).wait_recv()

    scaling = HD**-0.5
    scaling2 = scaling * 1.4426950408889634

    def compute(j):
        for band in range(BANDS):
            low, high = max(0, band - 1), min(BANDS, band + 2)
            tile_count = WT * (high - low)
            keys_count = tile_count * TILE
            q = qb[j, WT * band : WT * band + WT].reshape(ROWS, HD)
            g = gb[j, WT * band : WT * band + WT].reshape(ROWS, HD)
            ks = [kb[j, fr, WT * low : WT * high].reshape(keys_count, HD) for fr in range(3)]
            vs = [vb[j, fr, WT * low : WT * high].reshape(keys_count, HD) for fr in range(3)]
            scores = []
            for fr in range(3):
                start = fr * TILES + WT * low
                part = (dot_nt(ks[fr], q) * scaling2).reshape(tile_count, TILE, ROWS)
                part = part + bias[band, start : start + tile_count][:, None, :]
                scores.append(part.reshape(keys_count, ROWS))
            top = functools.reduce(
                jnp.maximum, [jnp.max(part, axis=0, keepdims=True) for part in scores]
            )
            weights = [jnp.exp2(part - top) for part in scores]
            total = sum(jnp.sum(part, axis=0, keepdims=True) for part in weights)
            share = 1.0 / total
            weights = [part * share for part in weights]
            probs = [part.astype(jnp.bfloat16) for part in weights]
            out = sum(dot_tn(probs[fr], vs[fr]) for fr in range(3)).astype(jnp.bfloat16)
            o_b[j, WT * band : WT * band + WT] = out.reshape(WT, TILE, HD)
            product = g.astype(jnp.float32) * out.astype(jnp.float32)
            deltas = jnp.sum(product.T, axis=0, keepdims=True)
            grads = []
            for fr in range(3):
                grad_prob = dot_nt(vs[fr], g)
                grads.append((weights[fr] * ((grad_prob - deltas) * scaling)).astype(jnp.bfloat16))
            dq = sum(dot_tn(grads[fr], ks[fr]) for fr in range(3)).astype(jnp.bfloat16)
            dq_b[j, WT * band : WT * band + WT] = dq.reshape(WT, TILE, HD)
            old = ROWS * (min(BANDS, band + 1) if band > 0 else 0)
            for fr in range(3):
                for acc, own, left, right in ((acc_k, own_k, grads, q), (acc_v, own_v, probs, g)):
                    into = own.at[j] if fr == 1 else acc.at[fr // 2]
                    part = dot_nn(left[fr], right)
                    seen = max(0, old - low * ROWS)
                    if seen:
                        into[low * ROWS : low * ROWS + seen, :] += part[:seen]
                    if seen < keys_count:
                        into[low * ROWS + seen : high * ROWS, :] = part[seen:]
        for side in range(2):
            send_k[j, side] = acc_k[side].astype(jnp.bfloat16).reshape(TILES, TILE, HD)
            send_v[j, side] = acc_v[side].astype(jnp.bfloat16).reshape(TILES, TILE, HD)

    def finish(j, half):
        part = pl.ds(2 * WT * half, 2 * WT)
        rows = pl.ds(pl.multiple_of(2 * ROWS * half, 2 * ROWS), 2 * ROWS)
        for own, back, out in ((own_k, back_k, dk_b), (own_v, back_v, dv_b)):
            full = own[j, rows].reshape(2 * WT, TILE, HD) + back[j, 0, part].astype(jnp.float32)
            out[j, part] = (full + back[j, 1, part].astype(jnp.float32)).astype(jnp.bfloat16)

    def share_out(j, carry):
        @pl.when(j < mine)
        def _():
            for n in range(BANDS):
                band = (2 * (x // 2) + n) % BANDS
                wait_in((0, 1), j, band)
                start_pieces(HALO, j, band)

        start_in((2, 3), j)
        return carry

    lax.fori_loop(0, most, share_out, 0)

    def attend(j, carry):
        for band in range(BANDS):
            wait_in((2, 3), j, band)
            wait_pieces(HALO, j, band)
        compute(j)
        start_pieces(RET, j, 1 - x // 2)
        start_pieces(RET, j, x // 2)
        start_out((0, 1), j, [(2 * (x // 2) + 2 + n) % BANDS for n in range(BANDS)])
        return carry

    lax.fori_loop(0, mine, attend, 0)

    def gather(j, carry):
        for part in (1 - x // 2, x // 2):
            wait_pieces(RET, j, part)
            finish(j, part)
            start_out((2, 3), j, (2 * part, 2 * part + 1))
        return carry

    lax.fori_loop(0, mine, gather, 0)

    for n in range(4):
        @pl.when(jnp.logical_not(self_attends(n)))
        def _():
            bias_copy(n).wait_send()

    def drain(j, carry):
        for n in range(4):
            @pl.when((j < head_count(n, x % 2)) & jnp.logical_not(self_attends(n)))
            def _():
                for arr in range(4):
                    in_copy(arr, j, n).wait_send()
                    out_arrival(arr, j, n).wait_recv()

            @pl.when((j < mine) & self_holds(n))
            def _():
                for arr in range(4):
                    out_own(arr, j).wait()

            @pl.when((j < mine) & jnp.logical_not(self_holds(n)))
            def _():
                for arr in range(4):
                    out_copy(arr, j, n).wait_send()

        @pl.when(j < mine)
        def _():
            for side in range(2):
                @pl.when(has[side])
                def _():
                    for arr in range(2):
                        for n in range(4):
                            piece(HALO, arr, j, side, n).wait_send()
                        for n in range(2):
                            piece(RET, arr, j, side, n).wait_send()

        return carry

    lax.fori_loop(0, most, drain, 0)


def copy_kernel(*refs):
    held, sems = refs[-2:]
    count = len(refs) // 2 - 1
    parts = [(i, t) for i in range(count) for t in range(WT)]
    loads = [pltpu.make_async_copy(refs[i].at[0, 0, t], held.at[i, t], sems.at[0, i, t]) for i, t in parts]
    stores = [pltpu.make_async_copy(held.at[i, t], refs[count + i].at[0, 0, t], sems.at[1, i, t]) for i, t in parts]
    for load in loads:
        load.start()
    for load, store in zip(loads, stores):
        load.wait()
        store.start()
    for store in stores:
        store.wait()


def on_device(frames, queries, keys, values, grad_out, windows):
    heads = queries.shape[-1] // HD
    most = (heads // 2 + 1) // 2
    near = (most, TILES, TILE, HD)
    wide = (most, 3, TILES, TILE, HD)
    both = (most, 2, TILES, TILE, HD)
    bf16 = functools.partial(pltpu.VMEM, dtype=jnp.bfloat16)
    f32 = functools.partial(pltpu.VMEM, dtype=jnp.float32)
    rows = TILES * TILE
    dma = pltpu.SemaphoreType.DMA
    anywhere = pl.BlockSpec(memory_space=pl.ANY)
    results = pl.pallas_call(
        functools.partial(kernel, frames, heads),
        name="window_attention",
        out_shape=[jax.ShapeDtypeStruct(queries.shape, jnp.bfloat16)] * 4,
        in_specs=[pl.BlockSpec(memory_space=pltpu.SMEM)] + [anywhere] * 4,
        out_specs=[anywhere] * 4,
        scratch_shapes=[
            bf16(near), bf16(near), bf16(wide), bf16(wide), f32((BANDS, 3 * TILES, ROWS)),
            f32((most, rows, HD)), f32((most, rows, HD)), f32((2, rows, HD)), f32((2, rows, HD)),
            bf16(both), bf16(both), bf16(both), bf16(both),
            bf16(near), bf16(near), bf16(near), bf16(near),
            dma((4, most, 4)), dma((4, most, 4)), dma((4, most)),
            dma((2, most, 2, 4)), dma((2, most, 2, 4)), dma((2, most, 2, 2)), dma((2, most, 2, 2)),
            dma((4, most, 4)), dma((4, most, 4)), dma((4, most)), dma((4,)), dma((4,)),
            f32((3 * TILES, ROWS)),
        ],
        cost_estimate=pl.CostEstimate(flops=8 * 10**9, bytes_accessed=8 * 10**6, transcendentals=4 * 10**6),
        compiler_params=pltpu.CompilerParams(
            collective_id=0, has_side_effects=True, vmem_limit_bytes=56 * 2**20
        ),
    )(windows, queries, keys, values, grad_out)
    return pl.pallas_call(
        copy_kernel,
        name="copy_out",
        out_shape=[jax.ShapeDtypeStruct(queries.shape, jnp.bfloat16)] * 4,
        in_specs=[anywhere] * 4,
        out_specs=[anywhere] * 4,
        scratch_shapes=[bf16((4, *queries.shape[2:])), dma((2, 4, WT))],
    )(*results)


def solution(mesh):
    placed = P("frame", "band", None, None, None)
    return jax.shard_map(
        functools.partial(on_device, mesh.shape["frame"]),
        mesh=mesh,
        in_specs=(placed, placed, placed, placed, P("frame", "band", None, None)),
        out_specs=(placed, placed, placed, placed),
        check_vma=False,
    )
```

time: 115 us -> 106 us (0.922)
  the two profiles are of different devices: /device:TPU:249 before, /device:TPU:9 now
where the time goes in v2:
time: 106 us
  Pallas kernels  105 us (99%)
    pallas_call x1, Pallas kernels, on_device(): pl.pallas_call(functools.partial(kernel, frames, heads), name='window_att...  102 us
    pallas_call x1, Pallas kernels, on_device(): pl.pallas_call(copy_kernel, name='copy_out', out_shape=[jax.ShapeDtypeStr...  2.89 us

profile of v2, /device:TPU:9, one launch (start us, length us, event | category | flops | bytes accessed | tf_op | source)
XLA Modules:
  0.0 105.8 jit_solution(17063289805416274184)
XLA Ops:
  0.6 102.2 %window_attention.1 = (bf16[1,1,2,64,3328]{4,3,2,1,0:T(8,128)(2,1)}, bf16[1,1,2,64,3328]{4,3,2,1,0:T(8,128)(2,1)}, bf16[1,1,2,64,3328]{4,3,2,1,0:T(8,128)(2,1)}, bf16[1,1,2,64,3328]{4,3,2,1,0:T(8,128)(2,1)}) custom-call(s32[1,1,2,8]{3,2,1,0:T(2,128)} %win_ref.1, bf16[1,1,2,64,3328]{4,3,2,1,0:T(8,128)(2,1)} %q_in.1, bf16[1,1,2,64,3328]{4,3,2,1,0:T(8,128)(2,1)} %k_in.1, ...), custom_call_target="tpu_custom_call" | custom-call | flops 8000000000 | bytes 8000000 | tf_op jit(solution)/shard_map/window_attention/pallas_call | solution.py:451
  102.9 2.9 %copy_out.1 = (bf16[1,1,2,64,3328]{4,3,2,1,0:T(8,128)(2,1)}, bf16[1,1,2,64,3328]{4,3,2,1,0:T(8,128)(2,1)}, bf16[1,1,2,64,3328]{4,3,2,1,0:T(8,128)(2,1)}, bf16[1,1,2,64,3328]{4,3,2,1,0:T(8,128)(2,1)}) custom-call(bf16[1,1,2,64,3328]{4,3,2,1,0:T(8,128)(2,1)} %get-tuple-element.8.refs_0_, bf16[1,1,2,64,3328]{4,3,2,1,0:T(8,128)(2,1)} %get-tuple-element.9.refs_1_, ...), custom_call_target="tpu_custom_call" | custom-call | tf_op jit(solution)/shard_map/copy_out/pallas_call | solution.py:472

commit v3 on v2

--- a/solution.py
+++ b/solution.py
@@ -15,7 +15,7 @@
 TILES = BANDS * WT
 ROWS = WT * TILE
 MASKED = -1e30
-AHEAD = 4
+AHEAD = 3
 HALO, RET = 0, 1
 
 
@@ -148,22 +148,23 @@
             ret_recv.at[arr, j, side],
         )
 
-    def piece(kind, arr, j, side, n):
+    def piece(kind, arr, j, side, n, straight=False):
         source, target, send, recv = side_refs(kind, arr, j, side)
         part = tiles(n) if kind == HALO else pl.ds(2 * WT * n, 2 * WT)
-        return pltpu.make_async_remote_copy(
-            src_ref=source.at[part], dst_ref=target.at[part], send_sem=send.at[n], recv_sem=recv.at[n],
+        source = in_refs[arr].at[0, 0, :, :, columns(x, j)] if straight else source.at[part]
+        return pltpu.make_async_remote_copy(
+            src_ref=source, dst_ref=target.at[part], send_sem=send.at[n], recv_sem=recv.at[n],
             device_id=to_side(side, j), device_id_type=MESH,
         )
 
     has = (has_prev, has_next)
 
-    def start_pieces(kind, j, n):
+    def start_pieces(kind, j, n, straight=False):
         for side in range(2):
             @pl.when(has[side])
             def _():
                 for arr in range(2):
-                    piece(kind, arr, j, side, n).start()
+                    piece(kind, arr, j, side, n, straight).start()
 
     def wait_pieces(kind, j, n):
         for side in range(2):
@@ -267,6 +268,12 @@
         pl.semaphore_wait(barrier, 9)
 
     start_in((0, 1), 0)
+
+    @pl.when(x % 2 == c)
+    def _():
+        start_pieces(HALO, 0, b, True)
+        start_pieces(HALO, 1, b, True)
+
     for n in range(4):
         @pl.when(jnp.logical_not(self_attends(n)))
         def _():
@@ -276,7 +283,8 @@
         def _():
             bias[b] = bias_own[...]
 
-    lax.fori_loop(1, most, lambda j, carry: (start_in((0, 1), j), carry)[1], 0)
+    for j in range(1, AHEAD):
+        start_in((0, 1), j)
 
     nothing = jnp.zeros((most, TILES, TILE, HD), jnp.bfloat16)
     for side in range(2):
@@ -355,9 +363,21 @@
             for n in range(BANDS):
                 band = (2 * (x // 2) + n) % BANDS
                 wait_in((0, 1), j, band)
-                start_pieces(HALO, j, band)
+
+                @pl.when(jnp.logical_not(self_holds(band)))
+                def _():
+                    start_pieces(HALO, j, band)
+
+        @pl.when(j + AHEAD < most)
+        def _():
+            start_in((0, 1), j + AHEAD)
 
         start_in((2, 3), j)
+
+        @pl.when((x % 2 == c) & (j + 2 < mine))
+        def _():
+            start_pieces(HALO, j + 2, b, True)
+
         return carry
 
     lax.fori_loop(0, most, share_out, 0)
@@ -374,52 +394,71 @@
 
     lax.fori_loop(0, mine, attend, 0)
 
+    def settle(arrs, j):
+        for n in range(4):
+            @pl.when((j < head_count(n, x % 2)) & jnp.logical_not(self_attends(n)))
+            def _():
+                for arr in arrs:
+                    out_arrival(arr, j, n).wait_recv()
+
+            @pl.when((j < mine) & self_holds(n))
+            def _():
+                for arr in arrs:
+                    out_own(arr, j).wait()
+
+            @pl.when((j < mine) & jnp.logical_not(self_holds(n)))
+            def _():
+                for arr in arrs:
+                    out_copy(arr, j, n).wait_send()
+
+    def settle_sides(kind, j):
+        for side in range(2):
+            @pl.when((j < mine) & has[side])
+            def _():
+                for arr in range(2):
+                    for n in range(4 if kind == HALO else 2):
+                        piece(kind, arr, j, side, n).wait_send()
+
+    def settle_in(j):
+        for n in range(4):
+            @pl.when((j < head_count(n, x % 2)) & jnp.logical_not(self_attends(n)))
+            def _():
+                for arr in range(4):
+                    in_copy(arr, j, n).wait_send()
+
     def gather(j, carry):
-        for part in (1 - x // 2, x // 2):
-            wait_pieces(RET, j, part)
-            finish(j, part)
-            start_out((2, 3), j, (2 * part, 2 * part + 1))
+        settle_in(j)
+        settle_sides(HALO, j)
+
+        @pl.when(j >= 1)
+        def _():
+            settle((0, 1), j - 1)
+
+        @pl.when(j >= 2)
+        def _():
+            settle((2, 3), j - 2)
+            settle_sides(RET, j - 2)
+
+        @pl.when(j < mine)
+        def _():
+            for part in (1 - x // 2, x // 2):
+                wait_pieces(RET, j, part)
+                finish(j, part)
+                start_out((2, 3), j, (2 * part, 2 * part + 1))
+
         return carry
 
-    lax.fori_loop(0, mine, gather, 0)
+    lax.fori_loop(0, most, gather, 0)
 
     for n in range(4):
         @pl.when(jnp.logical_not(self_attends(n)))
         def _():
             bias_copy(n).wait_send()
 
-    def drain(j, carry):
-        for n in range(4):
-            @pl.when((j < head_count(n, x % 2)) & jnp.logical_not(self_attends(n)))
-            def _():
-                for arr in range(4):
-                    in_copy(arr, j, n).wait_send()
-                    out_arrival(arr, j, n).wait_recv()
-
-            @pl.when((j < mine) & self_holds(n))
-            def _():
-                for arr in range(4):
-                    out_own(arr, j).wait()
-
-            @pl.when((j < mine) & jnp.logical_not(self_holds(n)))
-            def _():
-                for arr in range(4):
-                    out_copy(arr, j, n).wait_send()
-
-        @pl.when(j < mine)
-        def _():
-            for side in range(2):
-                @pl.when(has[side])
-                def _():
-                    for arr in range(2):
-                        for n in range(4):
-                            piece(HALO, arr, j, side, n).wait_send()
-                        for n in range(2):
-                            piece(RET, arr, j, side, n).wait_send()
-
-        return carry
-
-    lax.fori_loop(0, most, drain, 0)
+    settle((0, 1), most - 1)
+    for j in (most - 2, most - 1):
+        settle((2, 3), j)
+        settle_sides(RET, j)
 
 
 def copy_kernel(*refs):

time: 106 us -> 103 us (0.972)
  Pallas kernels: 105 us -> 102 us
    pallas_call x1, Pallas kernels: 102 us -> 99.1 us  [on_device(): pl.pallas_call(functools.partial(kernel, frames, heads), name='window_att...]
where the time goes in v3:
time: 103 us
  Pallas kernels  102 us (99%)
    pallas_call x1, Pallas kernels, on_device(): pl.pallas_call(functools.partial(kernel, frames, heads), name='window_att...  99.1 us
    pallas_call x1, Pallas kernels, on_device(): pl.pallas_call(copy_kernel, name='copy_out', out_shape=[jax.ShapeDtypeStr...  2.89 us

profile of v3, /device:TPU:9, one launch (start us, length us, event | category | flops | bytes accessed | tf_op | source)
XLA Modules:
  0.0 102.6 jit_solution(4934188531947339506)
XLA Ops:
  0.6 99.1 %window_attention.1 = (bf16[1,1,2,64,3328]{4,3,2,1,0:T(8,128)(2,1)}, bf16[1,1,2,64,3328]{4,3,2,1,0:T(8,128)(2,1)}, bf16[1,1,2,64,3328]{4,3,2,1,0:T(8,128)(2,1)}, bf16[1,1,2,64,3328]{4,3,2,1,0:T(8,128)(2,1)}) custom-call(s32[1,1,2,8]{3,2,1,0:T(2,128)} %win_ref.1, bf16[1,1,2,64,3328]{4,3,2,1,0:T(8,128)(2,1)} %q_in.1, bf16[1,1,2,64,3328]{4,3,2,1,0:T(8,128)(2,1)} %k_in.1, ...), custom_call_target="tpu_custom_call" | custom-call | flops 8000000000 | bytes 8000000 | tf_op jit(solution)/shard_map/window_attention/pallas_call | solution.py:490
  99.7 2.9 %copy_out.1 = (bf16[1,1,2,64,3328]{4,3,2,1,0:T(8,128)(2,1)}, bf16[1,1,2,64,3328]{4,3,2,1,0:T(8,128)(2,1)}, bf16[1,1,2,64,3328]{4,3,2,1,0:T(8,128)(2,1)}, bf16[1,1,2,64,3328]{4,3,2,1,0:T(8,128)(2,1)}) custom-call(bf16[1,1,2,64,3328]{4,3,2,1,0:T(8,128)(2,1)} %get-tuple-element.8.refs_0_, bf16[1,1,2,64,3328]{4,3,2,1,0:T(8,128)(2,1)} %get-tuple-element.9.refs_1_, ...), custom_call_target="tpu_custom_call" | custom-call | tf_op jit(solution)/shard_map/copy_out/pallas_call | solution.py:511

commit v4 on v3

--- a/solution.py
+++ b/solution.py
@@ -267,12 +267,16 @@
     def _():
         pl.semaphore_wait(barrier, 9)
 
-    start_in((0, 1), 0)
-
     @pl.when(x % 2 == c)
     def _():
         start_pieces(HALO, 0, b, True)
+
+    start_in((0, 1), 0)
+
+    @pl.when(x % 2 == c)
+    def _():
         start_pieces(HALO, 1, b, True)
+        start_pieces(HALO, 2, b, True)
 
     for n in range(4):
         @pl.when(jnp.logical_not(self_attends(n)))
@@ -374,9 +378,9 @@
 
         start_in((2, 3), j)
 
-        @pl.when((x % 2 == c) & (j + 2 < mine))
-        def _():
-            start_pieces(HALO, j + 2, b, True)
+        @pl.when((x % 2 == c) & (j + 3 < mine))
+        def _():
+            start_pieces(HALO, j + 3, b, True)
 
         return carry
 

time: 103 us -> 102 us (level)
  no operation moved by 1% of the time
where the time goes in v4:
time: 102 us
  Pallas kernels  101 us (99%)
    pallas_call x1, Pallas kernels, on_device(): pl.pallas_call(functools.partial(kernel, frames, heads), name='window_att...  98.4 us
    pallas_call x1, Pallas kernels, on_device(): pl.pallas_call(copy_kernel, name='copy_out', out_shape=[jax.ShapeDtypeStr...  2.89 us

profile of v4, /device:TPU:9, one launch (start us, length us, event | category | flops | bytes accessed | tf_op | source)
XLA Modules:
  0.0 101.9 jit_solution(7763493072582143013)
XLA Ops:
  0.6 98.4 %window_attention.1 = (bf16[1,1,2,64,3328]{4,3,2,1,0:T(8,128)(2,1)}, bf16[1,1,2,64,3328]{4,3,2,1,0:T(8,128)(2,1)}, bf16[1,1,2,64,3328]{4,3,2,1,0:T(8,128)(2,1)}, bf16[1,1,2,64,3328]{4,3,2,1,0:T(8,128)(2,1)}) custom-call(s32[1,1,2,8]{3,2,1,0:T(2,128)} %win_ref.1, bf16[1,1,2,64,3328]{4,3,2,1,0:T(8,128)(2,1)} %q_in.1, bf16[1,1,2,64,3328]{4,3,2,1,0:T(8,128)(2,1)} %k_in.1, ...), custom_call_target="tpu_custom_call" | custom-call | flops 8000000000 | bytes 8000000 | tf_op jit(solution)/shard_map/window_attention/pallas_call | solution.py:494
  99.0 2.9 %copy_out.1 = (bf16[1,1,2,64,3328]{4,3,2,1,0:T(8,128)(2,1)}, bf16[1,1,2,64,3328]{4,3,2,1,0:T(8,128)(2,1)}, bf16[1,1,2,64,3328]{4,3,2,1,0:T(8,128)(2,1)}, bf16[1,1,2,64,3328]{4,3,2,1,0:T(8,128)(2,1)}) custom-call(bf16[1,1,2,64,3328]{4,3,2,1,0:T(8,128)(2,1)} %get-tuple-element.8.refs_0_, bf16[1,1,2,64,3328]{4,3,2,1,0:T(8,128)(2,1)} %get-tuple-element.9.refs_1_, ...), custom_call_target="tpu_custom_call" | custom-call | tf_op jit(solution)/shard_map/copy_out/pallas_call | solution.py:515
